TPU v7x, 128 devices: a whole 4x4x4 slice. The times are simulated.
128 devices in a mesh: az: 32 (over y, x_hi, z), ax: 4 (over x_lo, core).
Axes of the slice: x: 4 (x_hi: 2, x_lo: 2; x = x_hi * 2 + x_lo), y: 4, z: 4, core: 2. Of those that a mesh axis runs over, the one named last changes fastest.
Arguments:
- start_field: float32 [16, 3, 64, 32, 512], P(None, None, 'az', 'ax'), may hold values from -4 to 4
- reluctivity: float32 [3, 64, 32, 512], P(None, 'az', 'ax'), may hold values from 0.05 to 1
- lamination: int32 [64, 32, 512], P('az', 'ax'), may hold values 0 or 1
- magnets: int32 [64, 32, 512], P('az', 'ax'), may hold values 0 or 1
- region_ids: int32 [64, 32, 512], P('az', 'ax'), may hold values from 0 to 127, as said below
- pieces: float32 [3, 16, 128], P(None, None, 'az'), may hold values from -5 to 5
- slot_map: int32 [16, 128], replicated, may hold values from 0 to 127, each once within a row
Outputs:
- solution_field: float32 [16, 3, 64, 32, 512], P(None, None, 'az', 'ax')
- residual: float32 [16, 3, 64, 32, 512], P(None, None, 'az', 'ax')
Inputs may be any that keep to these rules, and one draw needn't show every extreme that they name: `region_ids`: a cell of azimuthal sector s, the cells s * 2 to (s + 1) * 2 - 1 along the azimuth, holds a slot from s * 4 to (s + 1) * 4 - 1. `slot_map`: each row is a permutation.
All inputs are finite; a program needn't handle non-finite values. No bound on the sum of `lamination` or of `magnets` on one device may be relied on, other than what follows from the above.
Results may differ from a plain program's by a relative error of at most 0.00002.
Values sent between devices are 32-bit elements; how exact they have to be, the bound alone decides.
No kernel may reach another device: no remote copies, remote signals or barrier semaphores. Data moves between devices by JAX's collectives and lax.ppermute only.
A program may use at most 128 MiB of HBM per device.

v0:
```python
import jax
import jax.numpy as jnp
from jax import lax
from jax.sharding import PartitionSpec as P

mass_term = 1.0
cheb_centre = 8.5
cheb_halfwidth = 7.5
cheb_sigma = cheb_centre / cheb_halfwidth
rho_first = 1.0 / cheb_sigma
rho_second = 1.0 / (2.0 * cheb_sigma - rho_first)


def passed_along(value, axis, steps):
    count = lax.axis_size(axis)
    pairs = [(source, (source + steps) % count) for source in range(count)]
    return lax.ppermute(value, axis, pairs)


def from_behind(value, axis, steps):
    count = lax.axis_size(axis)
    first, last = (max(0, -steps), min(count, count - steps))
    return lax.ppermute(value, axis, [(source, source + steps) for source in range(first, last)])


def radial_forward(values):
    return jnp.concatenate([values[..., 1:], jnp.zeros_like(values[..., :1])], axis=-1) - values


def radial_backward(values):
    return values - jnp.concatenate([jnp.zeros_like(values[..., :1]), values[..., :-1]], axis=-1)


def curl_forward(core, along_a1, along_a2, along_z0, along_z2):
    return jnp.stack(
        [
            along_z2 - radial_forward(core[:, 1]),
            radial_forward(core[:, 0]) - along_a2,
            along_a1 - along_z0,
        ],
        axis=1,
    )


def curl_backward(core, along_a1, along_a2, along_z0, along_z2):
    return jnp.stack(
        [
            along_z2 - radial_backward(core[:, 1]),
            radial_backward(core[:, 0]) - along_a2,
            along_a1 - along_z0,
        ],
        axis=1,
    )


def residual_shifts(field, reluct, source):
    ahead_az = passed_along(field[:, 1:3, 0:1], "az", -1)
    ahead_ax = from_behind(jnp.stack([field[:, 0, :, 0:1], field[:, 2, :, 0:1]], axis=1), "ax", -1)
    step_az = jnp.concatenate([field[:, 1:3, 1:], ahead_az], axis=2) - field[:, 1:3]
    pair_field = jnp.stack([field[:, 0], field[:, 2]], axis=1)
    step_ax = jnp.concatenate([pair_field[:, :, :, 1:], ahead_ax], axis=3) - pair_field
    flux = curl_forward(field, step_az[:, 0], step_az[:, 1], step_ax[:, 0], step_ax[:, 1])
    intensity = reluct[None] * (flux - source)
    behind_az = passed_along(intensity[:, 1:3, -1:], "az", 1)
    behind_ax = from_behind(
        jnp.stack([intensity[:, 0, :, -1:], intensity[:, 2, :, -1:]], axis=1), "ax", 1
    )
    back_step_az = intensity[:, 1:3] - jnp.concatenate([behind_az, intensity[:, 1:3, :-1]], axis=2)
    pair_inten = jnp.stack([intensity[:, 0], intensity[:, 2]], axis=1)
    back_step_ax = pair_inten - jnp.concatenate([behind_ax, pair_inten[:, :, :, :-1]], axis=3)
    curl = curl_backward(
        intensity, back_step_az[:, 0], back_step_az[:, 1], back_step_ax[:, 0], back_step_ax[:, 1]
    )
    return -curl - mass_term * field


def shards(start_field, reluctivity, lamination, magnets, region_ids, pieces, slot_map):
    devs, comps, cells_az, cells_ax, radial = start_field.shape
    axial = jnp.array([0.0, 1.0, 0.0], jnp.float32)
    reluct = reluctivity * (
        1.0 + 3.0 * lamination.astype(jnp.float32)[None] * axial[:, None, None, None]
    )
    every_piece = lax.all_gather(pieces, "az", axis=2, tiled=True)
    slots_here = pieces.shape[2]
    base = lax.axis_index("az") * slots_here
    local_map = lax.dynamic_slice_in_dim(slot_map, base, slots_here, 1)
    local_table = jnp.take_along_axis(
        every_piece, jnp.broadcast_to(local_map[None], (comps, devs, slots_here)), axis=2
    )
    offset = (region_ids - base)[None, None]
    source = jnp.zeros(start_field.shape, jnp.float32)
    for slot in range(slots_here):
        values = jnp.transpose(local_table[:, :, slot])[:, :, None, None, None]
        source = jnp.where(offset == slot, values, source)
    source = source * magnets.astype(jnp.float32)[None, None]

    def residual_fn(field):
        return residual_shifts(field, reluct, source)

    first_res = residual_fn(start_field)
    first_dir = first_res / cheb_centre
    middle = start_field + first_dir
    second_res = residual_fn(middle)
    second_dir = rho_second * rho_first * first_dir + 2.0 * rho_second / cheb_halfwidth * second_res
    final = middle + second_dir
    return (final, residual_fn(final))


def solution(mesh):
    placed = (
        P(None, None, "az", "ax", None),
        P(None, "az", "ax", None),
        P("az", "ax", None),
        P("az", "ax", None),
        P("az", "ax", None),
        P(None, None, "az"),
        P(),
    )
    return jax.shard_map(
        shards,
        mesh=mesh,
        in_specs=placed,
        out_specs=(P(None, None, "az", "ax", None), P(None, None, "az", "ax", None)),
        check_vma=False,
    )
```

profile of v0, /device:TPU:1, one launch (start us, length us, event | category | flops | bytes accessed | tf_op | source)
XLA Modules:
  0.0 234.7 jit_solution(2493041710991904258)
XLA Ops:
  0.6 1.4 fusion.57
  2.0 0.8 pad_maximum_fusion.7
  2.8 3.3 %collective-permute-start = (f32[16,2,2,1,512]{4,3,2,0,1:T(1,128)}, f32[16,2,2,1,512]{4,3,2,0,1:T(1,128)S(1)}, u32[]{:S(2)}, u32[]{:S(2)}) collective-permute-start(f32[16,2,2,1,512]{4,3,2,0,1:T(1,128)} %pad_maximum_fusion.7), channel_id=1, source_target_pairs={{1,0},{2,1},{3,2},{5,4},{6,5},{7,6},{9,8},{10,9},{11,10},{13,12},{... | collective-permute-start | bytes 393224 | tf_op jit(solution)/shard_map/ppermute | solution.py:23
  6.1 2.3 fusion.56
  8.4 8.8 %collective-permute-start.1 = (f32[16,2,1,8,512]{4,3,2,0,1:T(8,128)}, f32[16,2,1,8,512]{4,3,2,0,1:T(8,128)}, u32[]{:S(2)}, u32[]{:S(2)}) collective-permute-start(f32[16,2,1,8,512]{4,3,2,0,1:T(8,128)} %get-tuple-element.77), channel_id=1, source_target_pairs={{0,124},{4,0},{8,4},{12,8},{16,12},{20,16},{24,20},{28,24},{32,28}... | collective-permute-start | bytes 1572872 | tf_op jit(solution)/shard_map/ppermute | solution.py:17
  17.2 1.1 slice_bitcast_fusion.17
  18.2 85.1 %all_gather.3 = f32[3,16,128]{1,0,2:T(4,128)S(1)} all-gather(f32[3,16,4]{1,0,2:T(4,128)S(1)} %copy.91), channel_id=1, replica_groups=mesh['az'=32,'ax'=4] {'az'}, dimensions={2}, use_global_device_ids=true | all-gather | bytes 25344 | tf_op jit(solution)/shard_map/all_gather | solution.py:83
  103.4 0.6 copy-done.5
  104.0 0.6 shift-left_or_fusion
  104.6 0.8 reshape.31
  105.4 2.1 gather_fusion
  107.7 0.7 fusion.45
  108.4 0.8 convert_multiply_fusion
  109.2 0.8 subtract_compare_fusion.3
  110.2 1.2 slice.393
  111.4 0.2 slice.394
  111.9 0.3 fusion.19
  112.2 0.7 copy-done.1
  112.9 1.3 slice_subtract_fusion.5
  114.3 0.4 fusion.43
  114.7 1.0 fusion
  116.0 15.4 %collective-permute-start.2 = (f32[16,2,2,1,512]{4,3,2,0,1:T(1,128)S(1)}, f32[16,2,2,1,512]{4,3,2,0,1:T(1,128)S(1)}, u32[]{:S(2)}, u32[]{:S(2)}) collective-permute-start(f32[16,2,2,1,512]{4,3,2,0,1:T(1,128)S(1)} %pad_maximum_fusion.8), channel_id=1, source_target_pairs={{0,1},{1,2},{2,3},{4,5},{5,6},{6,7},{8,9},{9,10},{10,11},{12,13},{... | collective-permute-start | bytes 393224 | tf_op jit(solution)/shard_map/ppermute | solution.py:23
  131.8 1.5 collective-permute-done.2
  133.3 0.4 fusion.17
  133.7 16.4 %collective-permute-done.3 = f32[16,2,1,8,512]{4,3,2,0,1:T(8,128)S(1)} collective-permute-done((f32[16,2,1,8,512]{4,3,2,0,1:T(8,128)S(1)}, f32[16,2,1,8,512]{4,3,2,0,1:T(8,128)S(1)}, u32[]{:S(2)}, u32[]{:S(2)}) %collective-permute-start.3) | collective-permute-done | bytes 524320 | tf_op jit(solution)/shard_map/ppermute | solution.py:17
  150.1 0.2 slice_subtract_fusion.4
  150.4 0.4 fusion.39
  150.8 0.4 multiply_add_fusion
  151.5 1.9 collective-permute-start.4
  153.5 0.2 slice_bitcast_fusion.11
  153.7 0.2 slice.429
  153.9 0.2 slice.430
  154.3 3.9 %collective-permute-done.4 = f32[16,2,2,1,512]{4,3,2,0,1:T(1,128)S(1)} collective-permute-done((f32[16,2,2,1,512]{4,3,2,0,1:T(1,128)S(1)}, f32[16,2,2,1,512]{4,3,2,0,1:T(1,128)S(1)}, u32[]{:S(2)}, u32[]{:S(2)}) %collective-permute-start.4) | collective-permute-done | bytes 131104 | tf_op jit(solution)/shard_map/ppermute | solution.py:23
  158.2 0.3 fusion.15
  158.5 8.5 %collective-permute-done.5 = f32[16,2,1,8,512]{4,3,2,0,1:T(8,128)S(1)} collective-permute-done((f32[16,2,1,8,512]{4,3,2,0,1:T(8,128)S(1)}, f32[16,2,1,8,512]{4,3,2,0,1:T(8,128)S(1)}, u32[]{:S(2)}, u32[]{:S(2)}) %collective-permute-start.5) | collective-permute-done | bytes 524320 | tf_op jit(solution)/shard_map/ppermute | solution.py:17
  167.0 0.2 slice_subtract_fusion.3
  167.3 0.4 fusion.35
  167.6 1.0 fusion.2
  169.0 1.9 collective-permute-start.6
  170.9 0.3 collective-permute-start.7
  171.5 1.4 collective-permute-done.6
  172.8 0.4 fusion.13
  173.2 16.7 %collective-permute-done.7 = f32[16,2,1,8,512]{4,3,2,0,1:T(8,128)S(1)} collective-permute-done((f32[16,2,1,8,512]{4,3,2,0,1:T(8,128)S(1)}, f32[16,2,1,8,512]{4,3,2,0,1:T(8,128)S(1)}, u32[]{:S(2)}, u32[]{:S(2)}) %collective-permute-start.7) | collective-permute-done | bytes 524320 | tf_op jit(solution)/shard_map/ppermute | solution.py:17
  189.8 0.2 slice_subtract_fusion.2
  190.1 0.4 fusion.31
  190.6 0.6 fusion.6
  191.5 3.3 %collective-permute-start.8 = (f32[16,2,2,1,512]{4,3,2,0,1:T(1,128)S(1)}, f32[16,2,2,1,512]{4,3,2,0,1:T(1,128)S(1)}, u32[]{:S(2)}, u32[]{:S(2)}) collective-permute-start(f32[16,2,2,1,512]{4,3,2,0,1:T(1,128)S(1)} %pad_maximum_fusion.11), channel_id=1, source_target_pairs={{1,0},{2,1},{3,2},{5,4},{6,5},{7,6},{9,8},{10,9},{11,10},{13,12},{... | collective-permute-start | bytes 393224 | tf_op jit(solution)/shard_map/ppermute | solution.py:23
  194.8 0.3 slice_bitcast_fusion.5
  195.1 0.2 slice.461
  195.3 0.2 slice.462
  195.7 2.4 %collective-permute-done.8 = f32[16,2,2,1,512]{4,3,2,0,1:T(1,128)S(1)} collective-permute-done((f32[16,2,2,1,512]{4,3,2,0,1:T(1,128)S(1)}, f32[16,2,2,1,512]{4,3,2,0,1:T(1,128)S(1)}, u32[]{:S(2)}, u32[]{:S(2)}) %collective-permute-start.8) | collective-permute-done | bytes 131104 | tf_op jit(solution)/shard_map/ppermute | solution.py:23
  198.0 0.3 fusion.11
  198.3 10.1 %collective-permute-done.9 = f32[16,2,1,8,512]{4,3,2,0,1:T(8,128)S(1)} collective-permute-done((f32[16,2,1,8,512]{4,3,2,0,1:T(8,128)S(1)}, f32[16,2,1,8,512]{4,3,2,0,1:T(8,128)S(1)}, u32[]{:S(2)}, u32[]{:S(2)}) %collective-permute-start.9) | collective-permute-done | bytes 524320 | tf_op jit(solution)/shard_map/ppermute | solution.py:17
  208.4 0.2 slice_subtract_fusion.1
  208.8 0.4 fusion.27
  209.2 1.0 fusion.7
  210.5 1.9 collective-permute-start.10
  212.5 0.3 slice_bitcast_fusion.2
  212.9 1.4 collective-permute-done.10
  214.3 0.3 copy_subtract_fusion
  214.7 16.5 %collective-permute-done.11 = f32[16,2,1,8,512]{4,3,2,0,1:T(8,128)S(1)} collective-permute-done((f32[16,2,1,8,512]{4,3,2,0,1:T(8,128)S(1)}, f32[16,2,1,8,512]{4,3,2,0,1:T(8,128)S(1)}, u32[]{:S(2)}, u32[]{:S(2)}) %collective-permute-start.11) | collective-permute-done | bytes 524320 | tf_op jit(solution)/shard_map/ppermute | solution.py:17
  231.2 0.2 slice_subtract_fusion
  231.5 0.4 fusion.23
  231.9 2.8 %fusion.8 = (f32[16,3,2,8,512]{4,3,2,1,0:T(8,128)}, f32[16,3,2,8,512]{4,3,2,1,0:T(8,128)}) fusion(f32[16,1,2,8,512]{4,3,2,1,0:T(8,128)S(1)} %slice_subtract_fusion.6, f32[16,1,2,8,512]{4,3,2,1,0:T(8,128)S(1)} %get-tuple-element.21, f32[16,1,2,8,512]{4,3,2,1,0:T(8,128)S(1)} %get-tuple-element.20, f32[16,1,2,8,512]{4,3,2,0,1:T(8,128)S(1)} %slice_subtract_fusion.8, ...), kind=kLoop, calls=%fused_computation.15 | loop fusion | flops 7077888 | bytes 9437184 | tf_op jit(solution)/shard_map/sub | solution.py:74
  (58 shorter events, 3.9 us)
Async XLA Ops:
  0.6 16.5 %copy-start = (f32[16,3,2,8,512]{4,3,2,1,0:T(8,128)S(1)}, f32[16,3,2,8,512]{4,3,2,1,0:T(8,128)}, u32[]{:S(2)}) copy-start(f32[16,3,2,8,512]{4,3,2,1,0:T(8,128)} %param.8) | copy-start | bytes 4718596
  2.8 109.1 %collective-permute-start = (f32[16,2,2,1,512]{4,3,2,0,1:T(1,128)}, f32[16,2,2,1,512]{4,3,2,0,1:T(1,128)S(1)}, u32[]{:S(2)}, u32[]{:S(2)}) collective-permute-start(f32[16,2,2,1,512]{4,3,2,0,1:T(1,128)} %pad_maximum_fusion.7), channel_id=1, source_target_pairs={{1,0},{2,1},{3,2},{5,4},{6,5},{7,6},{9,8},{10,9},{11,10},{13,12},{... | collective-permute-start | bytes 393224 | tf_op jit(solution)/shard_map/ppermute | solution.py:23
  8.4 9.8 %copy-start.7 = (f32[3,16,4]{1,2,0:T(4,128)S(1)}, f32[3,16,4]{1,2,0:T(4,128)}, u32[]{:S(2)}) copy-start(f32[3,16,4]{1,2,0:T(4,128)} %param.13) | copy-start | bytes 2308
  8.4 94.9 %copy-start.6 = (s32[16,128]{1,0:T(8,128)S(1)}, s32[16,128]{1,0:T(8,128)}, u32[]{:S(2)}) copy-start(s32[16,128]{1,0:T(8,128)} %param.14) | copy-start | bytes 24580
  8.4 103.8 %collective-permute-start.1 = (f32[16,2,1,8,512]{4,3,2,0,1:T(8,128)}, f32[16,2,1,8,512]{4,3,2,0,1:T(8,128)}, u32[]{:S(2)}, u32[]{:S(2)}) collective-permute-start(f32[16,2,1,8,512]{4,3,2,0,1:T(8,128)} %get-tuple-element.77), channel_id=1, source_target_pairs={{0,124},{4,0},{8,4},{12,8},{16,12},{20,16},{24,20},{28,24},{32,28}... | collective-permute-start | bytes 1572872 | tf_op jit(solution)/shard_map/ppermute | solution.py:17
  103.4 0.6 copy-start.5
  103.4 0.6 copy-start.3
  107.6 4.0 %copy-start.4 = (s32[2,8,512]{2,1,0:T(8,128)S(1)}, s32[2,8,512]{2,1,0:T(8,128)}, u32[]{:S(2)}) copy-start(s32[2,8,512]{2,1,0:T(8,128)} %param.11) | copy-start | bytes 98308
  107.6 4.0 %copy-start.2 = (f32[3,2,8,512]{3,2,1,0:T(8,128)S(1)}, f32[3,2,8,512]{3,2,1,0:T(8,128)}, u32[]{:S(2)}) copy-start(f32[3,2,8,512]{3,2,1,0:T(8,128)} %param.9) | copy-start | bytes 294916
  107.6 4.0 %copy-start.8 = (f32[3]{0:T(128)S(1)}, f32[3]{0:T(128)}, u32[]{:S(2)}) copy-start(f32[3]{0:T(128)} %constant.50.clone) | copy-start | bytes 40
  111.9 1.0 copy-start.1
  116.0 17.4 %collective-permute-start.2 = (f32[16,2,2,1,512]{4,3,2,0,1:T(1,128)S(1)}, f32[16,2,2,1,512]{4,3,2,0,1:T(1,128)S(1)}, u32[]{:S(2)}, u32[]{:S(2)}) collective-permute-start(f32[16,2,2,1,512]{4,3,2,0,1:T(1,128)S(1)} %pad_maximum_fusion.8), channel_id=1, source_target_pairs={{0,1},{1,2},{2,3},{4,5},{5,6},{6,7},{8,9},{9,10},{10,11},{12,13},{... | collective-permute-start | bytes 393224 | tf_op jit(solution)/shard_map/ppermute | solution.py:23
  131.4 18.7 %collective-permute-start.3 = (f32[16,2,1,8,512]{4,3,2,0,1:T(8,128)S(1)}, f32[16,2,1,8,512]{4,3,2,0,1:T(8,128)S(1)}, u32[]{:S(2)}, u32[]{:S(2)}) collective-permute-start(f32[16,2,1,8,512]{4,3,2,0,1:T(8,128)S(1)} %get-tuple-element.66), channel_id=1, source_target_pairs={{0,4},{4,8},{8,12},{12,16},{16,20},{20,24},{24,28},{28,32},{32,36}... | collective-permute-start | bytes 1572872 | tf_op jit(solution)/shard_map/ppermute | solution.py:17
  151.5 6.7 %collective-permute-start.4 = (f32[16,2,2,1,512]{4,3,2,0,1:T(1,128)S(1)}, f32[16,2,2,1,512]{4,3,2,0,1:T(1,128)S(1)}, u32[]{:S(2)}, u32[]{:S(2)}) collective-permute-start(f32[16,2,2,1,512]{4,3,2,0,1:T(1,128)S(1)} %pad_maximum_fusion.9), channel_id=1, source_target_pairs={{1,0},{2,1},{3,2},{5,4},{6,5},{7,6},{9,8},{10,9},{11,10},{13,12},{... | collective-permute-start | bytes 393224 | tf_op jit(solution)/shard_map/ppermute | solution.py:23
  153.4 13.6 %collective-permute-start.5 = (f32[16,2,1,8,512]{4,3,2,0,1:T(8,128)S(1)}, f32[16,2,1,8,512]{4,3,2,0,1:T(8,128)S(1)}, u32[]{:S(2)}, u32[]{:S(2)}) collective-permute-start(f32[16,2,1,8,512]{4,3,2,0,1:T(8,128)S(1)} %get-tuple-element.57), channel_id=1, source_target_pairs={{0,124},{4,0},{8,4},{12,8},{16,12},{20,16},{24,20},{28,24},{32,28}... | collective-permute-start | bytes 1572872 | tf_op jit(solution)/shard_map/ppermute | solution.py:17
  169.0 3.9 %collective-permute-start.6 = (f32[16,2,2,1,512]{4,3,2,0,1:T(1,128)S(1)}, f32[16,2,2,1,512]{4,3,2,0,1:T(1,128)S(1)}, u32[]{:S(2)}, u32[]{:S(2)}) collective-permute-start(f32[16,2,2,1,512]{4,3,2,0,1:T(1,128)S(1)} %pad_maximum_fusion.10), channel_id=1, source_target_pairs={{0,1},{1,2},{2,3},{4,5},{5,6},{6,7},{8,9},{9,10},{10,11},{12,13},{... | collective-permute-start | bytes 393224 | tf_op jit(solution)/shard_map/ppermute | solution.py:23
  170.9 19.0 %collective-permute-start.7 = (f32[16,2,1,8,512]{4,3,2,0,1:T(8,128)S(1)}, f32[16,2,1,8,512]{4,3,2,0,1:T(8,128)S(1)}, u32[]{:S(2)}, u32[]{:S(2)}) collective-permute-start(f32[16,2,1,8,512]{4,3,2,0,1:T(8,128)S(1)} %get-tuple-element.46), channel_id=1, source_target_pairs={{0,4},{4,8},{8,12},{12,16},{16,20},{20,24},{24,28},{28,32},{32,36}... | collective-permute-start | bytes 1572872 | tf_op jit(solution)/shard_map/ppermute | solution.py:17
  191.5 6.6 %collective-permute-start.8 = (f32[16,2,2,1,512]{4,3,2,0,1:T(1,128)S(1)}, f32[16,2,2,1,512]{4,3,2,0,1:T(1,128)S(1)}, u32[]{:S(2)}, u32[]{:S(2)}) collective-permute-start(f32[16,2,2,1,512]{4,3,2,0,1:T(1,128)S(1)} %pad_maximum_fusion.11), channel_id=1, source_target_pairs={{1,0},{2,1},{3,2},{5,4},{6,5},{7,6},{9,8},{10,9},{11,10},{13,12},{... | collective-permute-start | bytes 393224 | tf_op jit(solution)/shard_map/ppermute | solution.py:23
  194.7 13.7 %collective-permute-start.9 = (f32[16,2,1,8,512]{4,3,2,0,1:T(8,128)S(1)}, f32[16,2,1,8,512]{4,3,2,0,1:T(8,128)S(1)}, u32[]{:S(2)}, u32[]{:S(2)}) collective-permute-start(f32[16,2,1,8,512]{4,3,2,0,1:T(8,128)S(1)} %get-tuple-element.37), channel_id=1, source_target_pairs={{0,124},{4,0},{8,4},{12,8},{16,12},{20,16},{24,20},{28,24},{32,28}... | collective-permute-start | bytes 1572872 | tf_op jit(solution)/shard_map/ppermute | solution.py:17
  210.5 3.9 %collective-permute-start.10 = (f32[16,2,2,1,512]{4,3,2,0,1:T(1,128)S(1)}, f32[16,2,2,1,512]{4,3,2,0,1:T(1,128)S(1)}, u32[]{:S(2)}, u32[]{:S(2)}) collective-permute-start(f32[16,2,2,1,512]{4,3,2,0,1:T(1,128)S(1)} %pad_maximum_fusion.12), channel_id=1, source_target_pairs={{0,1},{1,2},{2,3},{4,5},{5,6},{6,7},{8,9},{9,10},{10,11},{12,13},{... | collective-permute-start | bytes 393224 | tf_op jit(solution)/shard_map/ppermute | solution.py:23
  212.4 18.8 %collective-permute-start.11 = (f32[16,2,1,8,512]{4,3,2,0,1:T(8,128)S(1)}, f32[16,2,1,8,512]{4,3,2,0,1:T(8,128)S(1)}, u32[]{:S(2)}, u32[]{:S(2)}) collective-permute-start(f32[16,2,1,8,512]{4,3,2,0,1:T(8,128)S(1)} %get-tuple-element.26), channel_id=1, source_target_pairs={{0,4},{4,8},{8,12},{12,16},{16,20},{20,24},{24,28},{28,32},{32,36}... | collective-permute-start | bytes 1572872 | tf_op jit(solution)/shard_map/ppermute | solution.py:17
where the time goes:
time: 235 us
  blocking collectives  85.1 us (36%)
  waiting for transfers between devices  78.6 us (33%)
  starting transfers between devices  37.1 us (16%)
  other arithmetic  19 us (8%)
  local copies, waits for them, and re-layouts  13.7 us (6%)
    all_gather x1, blocking collectives, shards(): every_piece = lax.all_gather(pieces, 'az', axis=2, tiled=True)  85.1 us
    ppermute x6, waiting for transfers between devices, passed_along(): return lax.ppermute(value, axis, pairs)  68.1 us
    ppermute x6, starting transfers between devices, from_behind(): lax.ppermute(value, axis, [(source, source + steps) for source in range(f...  27.8 us
    ppermute x6, waiting for transfers between devices, from_behind(): lax.ppermute(value, axis, [(source, source + steps) for source in range(f...  10.5 us
    ppermute x6, starting transfers between devices, passed_along(): return lax.ppermute(value, axis, pairs)  9.31 us
  transfers between devices with their start and end apart: 12, of which 10 were waited for; matrix products, arithmetic and copies ran while one was open for 7% of the time, Pallas kernels for 0%

commit v1 on v0

--- a/solution.py
+++ b/solution.py
@@ -80,7 +80,10 @@
     reluct = reluctivity * (
         1.0 + 3.0 * lamination.astype(jnp.float32)[None] * axial[:, None, None, None]
     )
-    every_piece = lax.all_gather(pieces, "az", axis=2, tiled=True)
+    size = lax.axis_size("az")
+    parts = jnp.stack([pieces for _ in range(size)])
+    parts = lax.all_to_all(parts, "az", split_axis=0, concat_axis=0)
+    every_piece = jnp.concatenate(parts, axis=2)
     slots_here = pieces.shape[2]
     base = lax.axis_index("az") * slots_here
     local_map = lax.dynamic_slice_in_dim(slot_map, base, slots_here, 1)

time: 235 us -> 150 us (0.64)
  blocking collectives: 85.1 us -> 0 us
  starting transfers between devices: 37.1 us -> 29.4 us
  waiting for transfers between devices: 78.6 us -> 82.3 us
  local copies, waits for them, and re-layouts: 13.7 us -> 16.1 us
    all_gather x1 -> x0, blocking collectives: 85.1 us -> none  [shards(): every_piece = lax.all_gather(pieces, 'az', axis=2, tiled=True)]
    ppermute x6, starting transfers between devices: 27.8 us -> 15.2 us  [from_behind(): lax.ppermute(value, axis, [(source, source + steps) for source in range(f...]
    all_to_all x0 -> x1, starting transfers between devices: none -> 4.52 us  [shards(): parts = lax.all_to_all(parts, 'az', split_axis=0, concat_axis=0)]
  transfers between devices with their start and end apart: 12 -> 13, of which waited for: 10 -> 11; matrix products, arithmetic and copies ran while one was open for 7% -> 13% of each run, Pallas kernels for 0% -> 0%
where the time goes in v1:
time: 150 us
  waiting for transfers between devices  82.3 us (55%)
  starting transfers between devices  29.4 us (20%)
  other arithmetic  20.5 us (14%)
  local copies, waits for them, and re-layouts  16.1 us (11%)
    ppermute x6, waiting for transfers between devices, passed_along(): return lax.ppermute(value, axis, pairs)  68.6 us
    ppermute x6, starting transfers between devices, from_behind(): lax.ppermute(value, axis, [(source, source + steps) for source in range(f...  15.2 us
    ppermute x6, waiting for transfers between devices, from_behind(): lax.ppermute(value, axis, [(source, source + steps) for source in range(f...  12.4 us
    ppermute x6, starting transfers between devices, passed_along(): return lax.ppermute(value, axis, pairs)  9.72 us
    all_to_all x1, starting transfers between devices, shards(): parts = lax.all_to_all(parts, 'az', split_axis=0, concat_axis=0)  4.52 us
  transfers between devices with their start and end apart: 13, of which 11 were waited for; matrix products, arithmetic and copies ran while one was open for 13% of the time, Pallas kernels for 0%

profile of v1, /device:TPU:1, one launch (start us, length us, event | category | flops | bytes accessed | tf_op | source)
XLA Modules:
  0.0 149.7 jit_solution(14004805324984308221)
XLA Ops:
  0.7 1.4 fusion.57
  2.2 3.3 %collective-permute-start = (f32[16,2,2,1,512]{4,3,2,0,1:T(1,128)S(1)}, f32[16,2,2,1,512]{4,3,2,0,1:T(1,128)S(1)}, u32[]{:S(2)}, u32[]{:S(2)}) collective-permute-start(f32[16,2,2,1,512]{4,3,2,0,1:T(1,128)S(1)} %pad_maximum_fusion.7), channel_id=1, source_target_pairs={{1,0},{2,1},{3,2},{5,4},{6,5},{7,6},{9,8},{10,9},{11,10},{13,12},{... | collective-permute-start | bytes 393224 | tf_op jit(solution)/shard_map/ppermute | solution.py:23
  5.5 2.3 %fusion.56 = (f32[16,2,1,8,512]{4,3,2,0,1:T(8,128)}, f32[16,2,1,8,512]{4,3,2,0,1:T(8,128)}) fusion(f32[16,3,2,8,512]{4,3,2,1,0:T(8,128)} %param.8), kind=kLoop, calls=%fused_computation.144 | loop fusion | bytes 2097152 | tf_op jit(solution)/shard_map/slice | solution.py:59
  7.8 8.8 %collective-permute-start.1 = (f32[16,2,1,8,512]{4,3,2,0,1:T(8,128)}, f32[16,2,1,8,512]{4,3,2,0,1:T(8,128)}, u32[]{:S(2)}, u32[]{:S(2)}) collective-permute-start(f32[16,2,1,8,512]{4,3,2,0,1:T(8,128)} %get-tuple-element.75), channel_id=1, source_target_pairs={{0,124},{4,0},{8,4},{12,8},{16,12},{20,16},{24,20},{28,24},{32,28}... | collective-permute-start | bytes 1572872 | tf_op jit(solution)/shard_map/ppermute | solution.py:17
  16.6 0.8 reshape.51
  17.4 4.5 %all-to-all-start = ((f32[32,1,192]{2,1,0:T(1,128)}), f32[32,1,192]{2,1,0:T(1,128)}, u32[]{:S(2)}, u32[]{:S(2)}) async-start(f32[32,1,192]{2,1,0:T(1,128)} %reshape.51), calls=%async_computation | async-start | bytes 65536 | tf_op jit(solution)/shard_map/all_to_all | solution.py:85
  22.0 1.1 slice_bitcast_fusion.17
  23.2 0.5 copy-done.12
  23.7 0.6 shift-left_or_fusion
  24.3 1.0 add_multiply_fusion
  25.3 1.1 fusion.18
  26.4 1.0 slice.393
  27.4 1.0 slice.394
  28.5 0.8 reshape.41
  29.3 1.4 all-to-all-done
  30.7 0.5 broadcast.111
  31.2 1.4 reduce.8
  32.8 2.0 %gather_fusion = f32[192]{0:T(256)S(1)} fusion(f32[3,16,128]{1,2,0:T(8,128)S(1)} %bitcast.167, s32[192]{0:T(256)S(1)} %reshape.41), kind=kCustom, calls=%fused_computation | custom fusion | bytes 3840 | tf_op jit(solution)/shard_map/jit(take_along_axis)/gather | solution.py:90
  35.1 1.6 %fusion.19 = f32[16,2,2,8,512]{4,3,2,0,1:T(8,128)S(1)} fusion(f32[16,1,2,8,512]{4,3,2,0,1:T(8,128)S(1)} %get-tuple-element.72, f32[16,1,2,8,512]{4,3,2,0,1:T(8,128)S(1)} %get-tuple-element.73, f32[16,2,2,1,512]{4,3,2,0,1:T(1,128)S(1)} %collective-permute-done, f32[16,2,2,7,512]{4,3,2,0,1:T(8,128)} %fusion.18), kind=kLoop, calls=%fused_computation.46 | loop fusion | flops 786432 | bytes 3145728 | tf_op jit(solution)/shard_map/sub | solution.py:61
  36.8 1.3 slice_subtract_fusion.5
  38.1 0.9 copy-done.5
  39.2 0.4 fusion.43
  39.6 1.0 fusion
  40.9 3.8 %collective-permute-start.2 = (f32[16,2,2,1,512]{4,3,2,0,1:T(1,128)S(1)}, f32[16,2,2,1,512]{4,3,2,0,1:T(1,128)S(1)}, u32[]{:S(2)}, u32[]{:S(2)}) collective-permute-start(f32[16,2,2,1,512]{4,3,2,0,1:T(1,128)S(1)} %pad_maximum_fusion.8), channel_id=1, source_target_pairs={{0,1},{1,2},{2,3},{4,5},{5,6},{6,7},{8,9},{9,10},{10,11},{12,13},{... | collective-permute-start | bytes 393224 | tf_op jit(solution)/shard_map/ppermute | solution.py:23
  44.7 0.5 collective-permute-start.3
  45.1 0.2 slice_bitcast_fusion.14
  45.5 1.1 collective-permute-done.2
  46.6 0.3 fusion.17
  46.9 17.0 %collective-permute-done.3 = f32[16,2,1,8,512]{4,3,2,0,1:T(8,128)S(1)} collective-permute-done((f32[16,2,1,8,512]{4,3,2,0,1:T(8,128)S(1)}, f32[16,2,1,8,512]{4,3,2,0,1:T(8,128)S(1)}, u32[]{:S(2)}, u32[]{:S(2)}) %collective-permute-start.3) | collective-permute-done | bytes 524320 | tf_op jit(solution)/shard_map/ppermute | solution.py:17
  63.9 0.2 slice_subtract_fusion.4
  64.2 0.4 fusion.39
  64.6 0.4 multiply_add_fusion
  65.3 1.9 %collective-permute-start.4 = (f32[16,2,2,1,512]{4,3,2,0,1:T(1,128)S(1)}, f32[16,2,2,1,512]{4,3,2,0,1:T(1,128)S(1)}, u32[]{:S(2)}, u32[]{:S(2)}) collective-permute-start(f32[16,2,2,1,512]{4,3,2,0,1:T(1,128)S(1)} %pad_maximum_fusion.9), channel_id=1, source_target_pairs={{1,0},{2,1},{3,2},{5,4},{6,5},{7,6},{9,8},{10,9},{11,10},{13,12},{... | collective-permute-start | bytes 393224 | tf_op jit(solution)/shard_map/ppermute | solution.py:23
  67.3 0.3 slice_bitcast_fusion.11
  68.2 5.2 %collective-permute-done.4 = f32[16,2,2,1,512]{4,3,2,0,1:T(1,128)S(1)} collective-permute-done((f32[16,2,2,1,512]{4,3,2,0,1:T(1,128)S(1)}, f32[16,2,2,1,512]{4,3,2,0,1:T(1,128)S(1)}, u32[]{:S(2)}, u32[]{:S(2)}) %collective-permute-start.4) | collective-permute-done | bytes 131104 | tf_op jit(solution)/shard_map/ppermute | solution.py:23
  73.4 0.3 fusion.15
  73.7 7.2 %collective-permute-done.5 = f32[16,2,1,8,512]{4,3,2,0,1:T(8,128)S(1)} collective-permute-done((f32[16,2,1,8,512]{4,3,2,0,1:T(8,128)S(1)}, f32[16,2,1,8,512]{4,3,2,0,1:T(8,128)S(1)}, u32[]{:S(2)}, u32[]{:S(2)}) %collective-permute-start.5) | collective-permute-done | bytes 524320 | tf_op jit(solution)/shard_map/ppermute | solution.py:17
  80.9 0.2 slice_subtract_fusion.3
  81.2 0.4 fusion.35
  81.6 1.0 fusion.2
  82.9 1.9 %collective-permute-start.6 = (f32[16,2,2,1,512]{4,3,2,0,1:T(1,128)S(1)}, f32[16,2,2,1,512]{4,3,2,0,1:T(1,128)S(1)}, u32[]{:S(2)}, u32[]{:S(2)}) collective-permute-start(f32[16,2,2,1,512]{4,3,2,0,1:T(1,128)S(1)} %pad_maximum_fusion.10), channel_id=1, source_target_pairs={{0,1},{1,2},{2,3},{4,5},{5,6},{6,7},{8,9},{9,10},{10,11},{12,13},{... | collective-permute-start | bytes 393224 | tf_op jit(solution)/shard_map/ppermute | solution.py:23
  84.9 0.3 collective-permute-start.7
  85.1 0.2 slice_bitcast_fusion.8
  85.5 1.3 collective-permute-done.6
  86.8 0.3 fusion.13
  87.1 18.7 %collective-permute-done.7 = f32[16,2,1,8,512]{4,3,2,0,1:T(8,128)S(1)} collective-permute-done((f32[16,2,1,8,512]{4,3,2,0,1:T(8,128)S(1)}, f32[16,2,1,8,512]{4,3,2,0,1:T(8,128)S(1)}, u32[]{:S(2)}, u32[]{:S(2)}) %collective-permute-start.7) | collective-permute-done | bytes 524320 | tf_op jit(solution)/shard_map/ppermute | solution.py:17
  105.8 0.2 slice_subtract_fusion.2
  106.1 0.4 fusion.31
  106.5 0.6 fusion.6
  107.4 2.3 %collective-permute-start.8 = (f32[16,2,2,1,512]{4,3,2,0,1:T(1,128)S(1)}, f32[16,2,2,1,512]{4,3,2,0,1:T(1,128)S(1)}, u32[]{:S(2)}, u32[]{:S(2)}) collective-permute-start(f32[16,2,2,1,512]{4,3,2,0,1:T(1,128)S(1)} %pad_maximum_fusion.11), channel_id=1, source_target_pairs={{1,0},{2,1},{3,2},{5,4},{6,5},{7,6},{9,8},{10,9},{11,10},{13,12},{... | collective-permute-start | bytes 393224 | tf_op jit(solution)/shard_map/ppermute | solution.py:23
  109.8 0.3 slice_bitcast_fusion.5
  110.7 3.3 %collective-permute-done.8 = f32[16,2,2,1,512]{4,3,2,0,1:T(1,128)S(1)} collective-permute-done((f32[16,2,2,1,512]{4,3,2,0,1:T(1,128)S(1)}, f32[16,2,2,1,512]{4,3,2,0,1:T(1,128)S(1)}, u32[]{:S(2)}, u32[]{:S(2)}) %collective-permute-start.8) | collective-permute-done | bytes 131104 | tf_op jit(solution)/shard_map/ppermute | solution.py:23
  114.0 0.3 fusion.11
  114.4 9.1 %collective-permute-done.9 = f32[16,2,1,8,512]{4,3,2,0,1:T(8,128)S(1)} collective-permute-done((f32[16,2,1,8,512]{4,3,2,0,1:T(8,128)S(1)}, f32[16,2,1,8,512]{4,3,2,0,1:T(8,128)S(1)}, u32[]{:S(2)}, u32[]{:S(2)}) %collective-permute-start.9) | collective-permute-done | bytes 524320 | tf_op jit(solution)/shard_map/ppermute | solution.py:17
  123.8 0.4 fusion.27
  124.1 1.0 fusion.7
  125.4 1.9 %collective-permute-start.10 = (f32[16,2,2,1,512]{4,3,2,0,1:T(1,128)S(1)}, f32[16,2,2,1,512]{4,3,2,0,1:T(1,128)S(1)}, u32[]{:S(2)}, u32[]{:S(2)}) collective-permute-start(f32[16,2,2,1,512]{4,3,2,0,1:T(1,128)S(1)} %pad_maximum_fusion.12), channel_id=1, source_target_pairs={{0,1},{1,2},{2,3},{4,5},{5,6},{6,7},{8,9},{9,10},{10,11},{12,13},{... | collective-permute-start | bytes 393224 | tf_op jit(solution)/shard_map/ppermute | solution.py:23
  127.4 0.2 slice_bitcast_fusion.2
  127.8 1.5 %collective-permute-done.10 = f32[16,2,2,1,512]{4,3,2,0,1:T(1,128)S(1)} collective-permute-done((f32[16,2,2,1,512]{4,3,2,0,1:T(1,128)S(1)}, f32[16,2,2,1,512]{4,3,2,0,1:T(1,128)S(1)}, u32[]{:S(2)}, u32[]{:S(2)}) %collective-permute-start.10) | collective-permute-done | bytes 131104 | tf_op jit(solution)/shard_map/ppermute | solution.py:23
  129.3 0.3 copy_subtract_fusion
  129.6 16.6 %collective-permute-done.11 = f32[16,2,1,8,512]{4,3,2,0,1:T(8,128)S(1)} collective-permute-done((f32[16,2,1,8,512]{4,3,2,0,1:T(8,128)S(1)}, f32[16,2,1,8,512]{4,3,2,0,1:T(8,128)S(1)}, u32[]{:S(2)}, u32[]{:S(2)}) %collective-permute-start.11) | collective-permute-done | bytes 524320 | tf_op jit(solution)/shard_map/ppermute | solution.py:17
  146.1 0.2 slice_subtract_fusion
  146.5 0.4 fusion.23
  146.9 2.8 %fusion.8 = (f32[16,3,2,8,512]{4,3,2,1,0:T(8,128)}, f32[16,3,2,8,512]{4,3,2,1,0:T(8,128)}) fusion(f32[16,1,2,8,512]{4,3,2,1,0:T(8,128)S(1)} %slice_subtract_fusion.6, f32[16,1,2,8,512]{4,3,2,1,0:T(8,128)S(1)} %get-tuple-element.19, f32[16,1,2,8,512]{4,3,2,1,0:T(8,128)S(1)} %get-tuple-element.18, f32[16,1,2,8,512]{4,3,2,0,1:T(8,128)S(1)} %slice_subtract_fusion.8, ...), kind=kLoop, calls=%fused_computation.15 | loop fusion | flops 7077888 | bytes 9437184 | tf_op jit(solution)/shard_map/sub | solution.py:74
  (77 shorter events, 4.8 us)
Async XLA Ops:
  0.6 15.9 %copy-start = (f32[3,16,4]{1,2,0:T(4,128)S(1)}, f32[3,16,4]{1,2,0:T(4,128)}, u32[]{:S(2)}) copy-start(f32[3,16,4]{1,2,0:T(4,128)} %param.13) | copy-start | bytes 2308
  0.6 21.3 %copy-start.2 = (f32[16,3,2,8,512]{4,3,2,1,0:T(8,128)S(1)}, f32[16,3,2,8,512]{4,3,2,1,0:T(8,128)}, u32[]{:S(2)}) copy-start(f32[16,3,2,8,512]{4,3,2,1,0:T(8,128)} %param.8) | copy-start | bytes 4718596
  2.2 33.0 %collective-permute-start = (f32[16,2,2,1,512]{4,3,2,0,1:T(1,128)S(1)}, f32[16,2,2,1,512]{4,3,2,0,1:T(1,128)S(1)}, u32[]{:S(2)}, u32[]{:S(2)}) collective-permute-start(f32[16,2,2,1,512]{4,3,2,0,1:T(1,128)S(1)} %pad_maximum_fusion.7), channel_id=1, source_target_pairs={{1,0},{2,1},{3,2},{5,4},{6,5},{7,6},{9,8},{10,9},{11,10},{13,12},{... | collective-permute-start | bytes 393224 | tf_op jit(solution)/shard_map/ppermute | solution.py:23
  7.8 28.9 %collective-permute-start.1 = (f32[16,2,1,8,512]{4,3,2,0,1:T(8,128)}, f32[16,2,1,8,512]{4,3,2,0,1:T(8,128)}, u32[]{:S(2)}, u32[]{:S(2)}) collective-permute-start(f32[16,2,1,8,512]{4,3,2,0,1:T(8,128)} %get-tuple-element.75), channel_id=1, source_target_pairs={{0,124},{4,0},{8,4},{12,8},{16,12},{20,16},{24,20},{28,24},{32,28}... | collective-permute-start | bytes 1572872 | tf_op jit(solution)/shard_map/ppermute | solution.py:17
  17.4 13.3 %all-to-all-start = ((f32[32,1,192]{2,1,0:T(1,128)}), f32[32,1,192]{2,1,0:T(1,128)}, u32[]{:S(2)}, u32[]{:S(2)}) async-start(f32[32,1,192]{2,1,0:T(1,128)} %reshape.51), calls=%async_computation | async-start | bytes 65536 | tf_op jit(solution)/shard_map/all_to_all | solution.py:85
  21.9 1.1 copy-start.14
  21.9 1.2 copy-start.9
  22.0 1.2 copy-start.10
  23.1 3.4 %copy-start.3 = (f32[16,2,8,512]{3,2,1,0:T(8,128)S(1)}, f32[16,2,8,512]{3,2,1,0:T(8,128)}, u32[]{:S(2)}) copy-start(f32[16,2,8,512]{3,2,1,0:T(8,128)} %get-tuple-element.70) | copy-start | bytes 1572868
  23.1 0.6 copy-start.12
  23.2 4.3 %copy-start.7 = (s32[16,4]{1,0:T(8,128)}, s32[16,4]{1,0:T(8,128)S(1)}, u32[]{:S(2)}) copy-start(s32[16,4]{1,0:T(8,128)S(1)} %broadcast_add_fusion) | copy-start | bytes 772
  26.4 2.0 %copy-start.11 = (s32[2,8,512]{2,1,0:T(8,128)S(1)}, s32[2,8,512]{2,1,0:T(8,128)}, u32[]{:S(2)}) copy-start(s32[2,8,512]{2,1,0:T(8,128)} %param.11) | copy-start | bytes 98308
  32.8 2.1 %copy-start.8 = (s32[16,4]{1,0:T(8,128)S(1)}, s32[16,4]{1,0:T(8,128)}, u32[]{:S(2)}) copy-start(s32[16,4]{1,0:T(8,128)} %copy-done.7) | copy-start | bytes 772
  32.8 2.1 %copy-start.13 = (pred[16,4]{1,0:T(8,128)(4,1)S(1)}, pred[16,4]{1,0:T(8,128)(4,1)}, u32[]{:S(2)}) copy-start(pred[16,4]{1,0:T(8,128)(4,1)} %copy-done.12) | copy-start | bytes 196
  35.1 1.6 %copy-start.4 = (f32[16,2,1,8,512]{4,3,2,0,1:T(8,128)S(1)}, f32[16,2,1,8,512]{4,3,2,0,1:T(8,128)}, u32[]{:S(2)}) copy-start(f32[16,2,1,8,512]{4,3,2,0,1:T(8,128)} %get-tuple-element.74) | copy-start | bytes 1572868
  38.0 1.0 copy-start.5
  38.0 1.2 copy-start.6
  40.9 5.7 %collective-permute-start.2 = (f32[16,2,2,1,512]{4,3,2,0,1:T(1,128)S(1)}, f32[16,2,2,1,512]{4,3,2,0,1:T(1,128)S(1)}, u32[]{:S(2)}, u32[]{:S(2)}) collective-permute-start(f32[16,2,2,1,512]{4,3,2,0,1:T(1,128)S(1)} %pad_maximum_fusion.8), channel_id=1, source_target_pairs={{0,1},{1,2},{2,3},{4,5},{5,6},{6,7},{8,9},{9,10},{10,11},{12,13},{... | collective-permute-start | bytes 393224 | tf_op jit(solution)/shard_map/ppermute | solution.py:23
  44.7 19.2 %collective-permute-start.3 = (f32[16,2,1,8,512]{4,3,2,0,1:T(8,128)S(1)}, f32[16,2,1,8,512]{4,3,2,0,1:T(8,128)S(1)}, u32[]{:S(2)}, u32[]{:S(2)}) collective-permute-start(f32[16,2,1,8,512]{4,3,2,0,1:T(8,128)S(1)} %get-tuple-element.64), channel_id=1, source_target_pairs={{0,4},{4,8},{8,12},{12,16},{16,20},{20,24},{24,28},{28,32},{32,36}... | collective-permute-start | bytes 1572872 | tf_op jit(solution)/shard_map/ppermute | solution.py:17
  65.3 8.1 %collective-permute-start.4 = (f32[16,2,2,1,512]{4,3,2,0,1:T(1,128)S(1)}, f32[16,2,2,1,512]{4,3,2,0,1:T(1,128)S(1)}, u32[]{:S(2)}, u32[]{:S(2)}) collective-permute-start(f32[16,2,2,1,512]{4,3,2,0,1:T(1,128)S(1)} %pad_maximum_fusion.9), channel_id=1, source_target_pairs={{1,0},{2,1},{3,2},{5,4},{6,5},{7,6},{9,8},{10,9},{11,10},{13,12},{... | collective-permute-start | bytes 393224 | tf_op jit(solution)/shard_map/ppermute | solution.py:23
  67.3 13.6 %collective-permute-start.5 = (f32[16,2,1,8,512]{4,3,2,0,1:T(8,128)S(1)}, f32[16,2,1,8,512]{4,3,2,0,1:T(8,128)S(1)}, u32[]{:S(2)}, u32[]{:S(2)}) collective-permute-start(f32[16,2,1,8,512]{4,3,2,0,1:T(8,128)S(1)} %get-tuple-element.55), channel_id=1, source_target_pairs={{0,124},{4,0},{8,4},{12,8},{16,12},{20,16},{24,20},{28,24},{32,28}... | collective-permute-start | bytes 1572872 | tf_op jit(solution)/shard_map/ppermute | solution.py:17
  82.9 3.9 %collective-permute-start.6 = (f32[16,2,2,1,512]{4,3,2,0,1:T(1,128)S(1)}, f32[16,2,2,1,512]{4,3,2,0,1:T(1,128)S(1)}, u32[]{:S(2)}, u32[]{:S(2)}) collective-permute-start(f32[16,2,2,1,512]{4,3,2,0,1:T(1,128)S(1)} %pad_maximum_fusion.10), channel_id=1, source_target_pairs={{0,1},{1,2},{2,3},{4,5},{5,6},{6,7},{8,9},{9,10},{10,11},{12,13},{... | collective-permute-start | bytes 393224 | tf_op jit(solution)/shard_map/ppermute | solution.py:23
  84.9 20.9 %collective-permute-start.7 = (f32[16,2,1,8,512]{4,3,2,0,1:T(8,128)S(1)}, f32[16,2,1,8,512]{4,3,2,0,1:T(8,128)S(1)}, u32[]{:S(2)}, u32[]{:S(2)}) collective-permute-start(f32[16,2,1,8,512]{4,3,2,0,1:T(8,128)S(1)} %get-tuple-element.44), channel_id=1, source_target_pairs={{0,4},{4,8},{8,12},{12,16},{16,20},{20,24},{24,28},{28,32},{32,36}... | collective-permute-start | bytes 1572872 | tf_op jit(solution)/shard_map/ppermute | solution.py:17
  107.4 6.6 %collective-permute-start.8 = (f32[16,2,2,1,512]{4,3,2,0,1:T(1,128)S(1)}, f32[16,2,2,1,512]{4,3,2,0,1:T(1,128)S(1)}, u32[]{:S(2)}, u32[]{:S(2)}) collective-permute-start(f32[16,2,2,1,512]{4,3,2,0,1:T(1,128)S(1)} %pad_maximum_fusion.11), channel_id=1, source_target_pairs={{1,0},{2,1},{3,2},{5,4},{6,5},{7,6},{9,8},{10,9},{11,10},{13,12},{... | collective-permute-start | bytes 393224 | tf_op jit(solution)/shard_map/ppermute | solution.py:23
  109.7 13.7 %collective-permute-start.9 = (f32[16,2,1,8,512]{4,3,2,0,1:T(8,128)S(1)}, f32[16,2,1,8,512]{4,3,2,0,1:T(8,128)S(1)}, u32[]{:S(2)}, u32[]{:S(2)}) collective-permute-start(f32[16,2,1,8,512]{4,3,2,0,1:T(8,128)S(1)} %get-tuple-element.35), channel_id=1, source_target_pairs={{0,124},{4,0},{8,4},{12,8},{16,12},{20,16},{24,20},{28,24},{32,28}... | collective-permute-start | bytes 1572872 | tf_op jit(solution)/shard_map/ppermute | solution.py:17
  125.4 3.9 %collective-permute-start.10 = (f32[16,2,2,1,512]{4,3,2,0,1:T(1,128)S(1)}, f32[16,2,2,1,512]{4,3,2,0,1:T(1,128)S(1)}, u32[]{:S(2)}, u32[]{:S(2)}) collective-permute-start(f32[16,2,2,1,512]{4,3,2,0,1:T(1,128)S(1)} %pad_maximum_fusion.12), channel_id=1, source_target_pairs={{0,1},{1,2},{2,3},{4,5},{5,6},{6,7},{8,9},{9,10},{10,11},{12,13},{... | collective-permute-start | bytes 393224 | tf_op jit(solution)/shard_map/ppermute | solution.py:23
  127.4 18.8 %collective-permute-start.11 = (f32[16,2,1,8,512]{4,3,2,0,1:T(8,128)S(1)}, f32[16,2,1,8,512]{4,3,2,0,1:T(8,128)S(1)}, u32[]{:S(2)}, u32[]{:S(2)}) collective-permute-start(f32[16,2,1,8,512]{4,3,2,0,1:T(8,128)S(1)} %get-tuple-element.24), channel_id=1, source_target_pairs={{0,4},{4,8},{8,12},{12,16},{16,20},{20,24},{24,28},{28,32},{32,36}... | collective-permute-start | bytes 1572872 | tf_op jit(solution)/shard_map/ppermute | solution.py:17
  146.9 2.8 %copy-start.1 = (f32[3,16,4]{1,2,0:T(4,128)S(1)}, f32[3,16,4]{1,2,0:T(4,128)}, u32[]{:S(2)}) copy-start(f32[3,16,4]{1,2,0:T(4,128)} %param.13) | copy-start | bytes 2308
